TPU v7x, 512 devices: a whole 4x4x16 slice. The times are simulated.
512 devices in a mesh: shape: 16 (over z_lo, x), query: 32 (over z_hi, y, core).
Axes of the slice: x: 4, y: 4, z: 16 (z_hi: 4, z_lo: 4; z = z_hi * 4 + z_lo), core: 2. Of those that a mesh axis runs over, the one named last changes fastest.
Arguments:
- queries: bfloat16 [16, 4096, 512], P('shape', 'query'), may hold values from -128 to 128
- keys: bfloat16 [16, 1024, 512], P('shape', 'query'), may hold values from -5 to 5
- values: bfloat16 [16, 1024, 512], P('shape', 'query'), may hold values from -6 to 6
- out_weight: bfloat16 [512, 512], replicated, may hold values from -0.25 to 0.25
- out_grad: float32 [16, 4096, 512], P('shape', 'query'), may hold values from -6 to 6
Outputs:
- query_grad: float32 [16, 4096, 512], P('shape', 'query')
- key_grad: float32 [16, 1024, 512], P('shape', 'query')
- value_grad: float32 [16, 1024, 512], P('shape', 'query')
- weight_grad: float32 [512, 512], replicated
All inputs are finite; a program needn't handle non-finite values.
Results may differ from a plain program's by a relative error of at most 0.02.
Values may be sent and summed in bfloat16 or wider, within the bound.
A program may use at most 64 MiB of HBM per device.

v0:
```python
import math
import jax
import jax.numpy as jnp
from jax import lax
from jax.sharding import PartitionSpec as P

HEADS = 8
HEAD = 64


def shards(queries, keys, values, out_weight, out_grad):
    lat_rows = keys.shape[1]
    width = queries.shape[2]
    scale = 1.0 / math.sqrt(HEAD)
    shape_count = lax.axis_size("shape")
    members = lax.axis_size("query")
    query_rows = queries[0]
    grad_b = out_grad[0].astype(jnp.bfloat16)
    d_attn = jnp.einsum("tf,df->td", grad_b, out_weight, preferred_element_type=jnp.float32).astype(
        jnp.bfloat16
    )
    key_all, value_all = (
        lax.all_gather(keys[0], "query", axis=0, tiled=True),
        lax.all_gather(values[0], "query", axis=0, tiled=True),
    )
    grad_list, attn_list, key_list, value_list = ([], [], [], [])
    for head_index in range(HEADS):
        cols = slice(head_index * HEAD, (head_index + 1) * HEAD)
        q_head = query_rows[:, cols]
        key_head = key_all[:, cols]
        value_head = value_all[:, cols]
        scores = jnp.dot(q_head, key_head.T, preferred_element_type=jnp.float32) * scale
        top = jnp.max(scores, axis=1, keepdims=True)
        lse = top + jnp.log(jnp.sum(jnp.exp(scores - top), axis=1, keepdims=True))
        probs = jnp.exp(scores - lse)
        probs_b = probs.astype(jnp.bfloat16)
        attn_b = jnp.dot(probs_b, value_head, preferred_element_type=jnp.float32).astype(
            jnp.bfloat16
        )
        d_head = d_attn[:, cols]
        delta = jnp.sum(
            d_head.astype(jnp.float32) * attn_b.astype(jnp.float32), axis=1, keepdims=True
        )
        d_probs = jnp.dot(d_head, value_head.T, preferred_element_type=jnp.float32)
        d_scores = (probs * (d_probs - delta) * scale).astype(jnp.bfloat16)
        grad_list.append(jnp.dot(d_scores, key_head, preferred_element_type=jnp.float32))
        key_list.append(
            jnp.einsum("tm,td->md", d_scores, q_head, preferred_element_type=jnp.float32)
        )
        value_list.append(
            jnp.einsum("tm,td->md", probs_b, d_head, preferred_element_type=jnp.float32)
        )
        attn_list.append(attn_b)
    query_grad = jnp.concatenate(grad_list, axis=1)
    attn = jnp.concatenate(attn_list, axis=1)
    key_terms = jnp.concatenate(key_list, axis=1).reshape(members, lat_rows, width)
    value_terms = jnp.concatenate(value_list, axis=1).reshape(members, lat_rows, width)
    key_in, value_in = (
        lax.all_to_all(key_terms, "query", split_axis=0, concat_axis=0, tiled=True),
        lax.all_to_all(value_terms, "query", split_axis=0, concat_axis=0, tiled=True),
    )
    key_grad = jnp.sum(key_in, axis=0)
    value_grad = jnp.sum(value_in, axis=0)
    weight_term = jnp.einsum("td,tf->df", attn, grad_b, preferred_element_type=jnp.float32) * (
        1.0 / shape_count
    )
    weight_grad = lax.psum(weight_term, ("shape", "query"))
    return (query_grad[None], key_grad[None], value_grad[None], weight_grad)


def solution(mesh):
    return jax.shard_map(
        shards,
        mesh=mesh,
        in_specs=(
            P("shape", "query", None),
            P("shape", "query", None),
            P("shape", "query", None),
            P(),
            P("shape", "query", None),
        ),
        out_specs=(
            P("shape", "query", None),
            P("shape", "query", None),
            P("shape", "query", None),
            P(),
        ),
        check_vma=False,
    )
```

profile of v0, /device:TPU:1, one launch (start us, length us, event | category | flops | bytes accessed | tf_op | source)
XLA Modules:
  0.0 804.2 jit_solution(14749125188669435958)
XLA Ops:
  8.2 1.3 convolution_convert_fusion
  9.5 79.2 %all-gather.5.cloned.1.call-done = bf16[1,1024,512]{2,1,0:T(8,128)(2,1)} async-done(((bf16[1,32,512]{2,1,0:T(8,128)(2,1)}), bf16[1,1024,512]{2,1,0:T(8,128)(2,1)}) %all-gather.5.cloned.1.call-update) | async-done | bytes 1048592 | tf_op jit(solution)/shard_map/all_gather | solution.py:23
  88.7 1.4 fusion.117
  90.1 1.6 fusion.118
  91.6 1.5 fusion.119
  100.0 1.0 convolution_dynamic-update-slice_fusion.4
  102.0 1.0 convolution_dynamic-update-slice_fusion.2
  105.0 2.9 copy.27
  107.9 7.5 all-to-all-start.1
  116.1 140.1 %all-gather.7.cloned.1.call-done = bf16[1,1024,512]{2,1,0:T(8,128)(2,1)} async-done(((bf16[1,32,512]{2,1,0:T(8,128)(2,1)}), bf16[1,1024,512]{2,1,0:T(8,128)(2,1)}) %all-gather.7.cloned.1.call-update) | async-done | bytes 1048592 | tf_op jit(solution)/shard_map/all_gather | solution.py:24
  256.3 1.4 convolution_convert_fusion.2
  257.7 1.3 convolution_convert_fusion.3
  259.1 1.3 convolution_convert_fusion.4
  267.5 1.0 convolution_dynamic-update-slice_fusion.12
  272.6 1.0 convolution_dynamic-update-slice_fusion.8
  273.6 2.9 copy.26
  276.7 7.6 all-to-all-start
  284.8 2.3 convolution_multiply_fusion
  290.4 1.8 copy.28
  292.2 2.4 reduce_sum.179
  294.5 90.0 %all-to-all-done = f32[32,32,512]{2,1,0:T(8,128)} async-done(((f32[32,32,512]{2,1,0:T(8,128)}), f32[32,32,512]{2,1,0:T(8,128)}, u32[]{:S(2)}, u32[]{:S(2)}) %all-to-all-start) | async-done | bytes 2097184 | tf_op jit(solution)/shard_map/all_to_all | solution.py:59
  384.6 2.4 reduce_sum.178
  386.9 408.5 %all-reduce.2.cloned.1.call-done = f32[512,512]{1,0:T(8,128)} async-done(((f32[512,512]{1,0:T(8,128)}), f32[512,512]{1,0:T(8,128)}) %all-reduce.2.cloned.1.call-update) | async-done | bytes 1048592 | tf_op jit(solution)/shard_map/psum | solution.py:67
  795.4 2.3 copy.59
  (158 shorter events, 26.0 us)
Async XLA Ops:
  7.2 84.4 %copy-start.23 = (bf16[1,128,512]{2,1,0:T(8,128)(2,1)S(1)}, bf16[1,128,512]{2,1,0:T(8,128)(2,1)}, u32[]{:S(2)}) copy-start(bf16[1,128,512]{2,1,0:T(8,128)(2,1)} %param.5) | copy-start | bytes 393220
  7.2 81.5 %all-gather.5.cloned.1.call-start = ((), (), s32[]{:S(2)}) async-start(), calls=%async_computation.3 | async-start | bytes 1081344 | tf_op jit(solution)/shard_map/all_gather | solution.py:23
  90.0 6.9 copy-start.9
  91.6 6.4 copy-start.7
  93.1 5.9 copy-start.5
  93.5 6.5 copy-start.3
  95.0 9.0 %copy-start.11 = (f32[128,1024]{1,0:T(8,128)}, f32[128,1024]{1,0:T(8,128)S(1)}, u32[]{:S(2)}) copy-start(f32[128,1024]{1,0:T(8,128)S(1)} %get-tuple-element.21) | copy-start | bytes 1572868
  95.2 166.2 %copy-start.43 = (f32[128]{0:T(128)}, f32[128]{0:T(128)S(1)}, u32[]{:S(2)}) copy-start(f32[128]{0:T(128)S(1)} %log_add_fusion.7) | copy-start | bytes 1540
  95.5 165.6 %copy-start.44 = (f32[128]{0:T(128)}, f32[128]{0:T(128)S(1)}, u32[]{:S(2)}) copy-start(f32[128]{0:T(128)S(1)} %log_add_fusion.6) | copy-start | bytes 1540
  95.7 165.0 %copy-start.41 = (f32[128]{0:T(128)}, f32[128]{0:T(128)S(1)}, u32[]{:S(2)}) copy-start(f32[128]{0:T(128)S(1)} %log_add_fusion.5) | copy-start | bytes 1540
  97.0 164.8 %copy-start.46 = (f32[128]{0:T(128)}, f32[128]{0:T(128)S(1)}, u32[]{:S(2)}) copy-start(f32[128]{0:T(128)S(1)} %log_add_fusion) | copy-start | bytes 1540
  107.9 168.7 %all-to-all-start.1 = ((f32[32,32,512]{2,1,0:T(8,128)}), f32[32,32,512]{2,1,0:T(8,128)}, u32[]{:S(2)}, u32[]{:S(2)}) async-start(f32[32,32,512]{2,1,0:T(8,128)} %bitcast.63), calls=%async_computation.1 | async-start | bytes 4194304 | tf_op jit(solution)/shard_map/all_to_all | solution.py:60
  115.4 140.9 %all-gather.7.cloned.1.call-start = ((), (), s32[]{:S(2)}) async-start(), calls=%async_computation.4 | async-start | bytes 1081344 | tf_op jit(solution)/shard_map/all_gather | solution.py:24
  256.3 4.8 copy-start.8
  276.6 8.0 copy-start.27
  276.6 8.0 copy-start.29
  276.6 8.0 copy-start.31
  276.6 8.0 copy-start.33
  276.6 8.0 copy-start.35
  276.6 8.0 copy-start.37
  276.6 8.0 copy-start.39
  276.6 8.0 copy-start.40
  276.7 107.9 %all-to-all-start = ((f32[32,32,512]{2,1,0:T(8,128)}), f32[32,32,512]{2,1,0:T(8,128)}, u32[]{:S(2)}, u32[]{:S(2)}) async-start(f32[32,32,512]{2,1,0:T(8,128)} %bitcast.64), calls=%async_computation | async-start | bytes 4194304 | tf_op jit(solution)/shard_map/all_to_all | solution.py:59
  284.3 511.1 %all-reduce.2.cloned.1.call-start = ((), (), s32[]{:S(2)}) async-start(), calls=%async_computation.2 | async-start | bytes 2097152 | tf_op jit(solution)/shard_map/psum | solution.py:67
  (29 other events, 98.1 us)
Sparse Core Ops, SparseCore 0:
  11.2 77.4 all-gather.4
  119.4 136.8 all-gather.6
  291.2 504.1 all-reduce.1
where the time goes:
time: 805 us; the launch traced here: 804 us
  waiting for transfers between devices  719 us (89%)
  matrix products  37.1 us (5%)
  starting transfers between devices  15.4 us (2%)
  between operations  14.6 us (2%)
  local copies, waits for them, and re-layouts  11.2 us (1%)
    psum x1, waiting for transfers between devices, shards(): weight_grad = lax.psum(weight_term, ('shape', 'query'))  408 us
    all_gather x1, waiting for transfers between devices, shards(): lax.all_gather(values[0], 'query', axis=0, tiled=True)  140 us
    all_to_all x1, waiting for transfers between devices, shards(): lax.all_to_all(key_terms, 'query', split_axis=0, concat_axis=0, tiled=True)  90 us
    all_gather x1, waiting for transfers between devices, shards(): lax.all_gather(keys[0], 'query', axis=0, tiled=True)  79.2 us
  transfers between devices with their start and end apart: 5, of which 4 were waited for; matrix products, arithmetic and copies ran while one was open for 4% of the time, Pallas kernels for 0%

commit v1 on v0

--- a/solution.py
+++ b/solution.py
@@ -64,7 +64,7 @@
     weight_term = jnp.einsum("td,tf->df", attn, grad_b, preferred_element_type=jnp.float32) * (
         1.0 / shape_count
     )
-    weight_grad = lax.psum(weight_term, ("shape", "query"))
+    weight_grad = lax.psum(lax.psum(weight_term, "query"), "shape")
     return (query_grad[None], key_grad[None], value_grad[None], weight_grad)
 
 

time: 805 us -> 891 us (1.11); the launches traced: 804 us -> 881 us
  waiting for transfers between devices: 719 us -> 793 us
    psum x1 -> x2, waiting for transfers between devices: 408 us -> 573 us  [shards(): weight_grad = lax.psum(lax.psum(weight_term, 'query'), 'shape')]
    all_to_all x1, waiting for transfers between devices: 90 us -> 0.01 us  [shards(): lax.all_to_all(key_terms, 'query', split_axis=0, concat_axis=0, tiled=True)]
  transfers between devices with their start and end apart: 5 -> 6, of which waited for: 4 -> 4; matrix products, arithmetic and copies ran while one was open for 4% -> 4% of each run, Pallas kernels for 0% -> 0%
where the time goes in v1:
time: 891 us; the launch traced here: 881 us
  waiting for transfers between devices  793 us (89%)
  matrix products  40.3 us (5%)
  starting transfers between devices  15.3 us (2%)
  between operations  14.5 us (2%)
  local copies, waits for them, and re-layouts  10.5 us (1%)
    psum x2, waiting for transfers between devices, shards(): weight_grad = lax.psum(lax.psum(weight_term, 'query'), 'shape')  573 us
    all_gather x1, waiting for transfers between devices, shards(): lax.all_gather(values[0], 'query', axis=0, tiled=True)  140 us
    all_gather x1, waiting for transfers between devices, shards(): lax.all_gather(keys[0], 'query', axis=0, tiled=True)  79.2 us
  transfers between devices with their start and end apart: 6, of which 4 were waited for; matrix products, arithmetic and copies ran while one was open for 4% of the time, Pallas kernels for 0%

profile of v1, /device:TPU:1, one launch (start us, length us, event | category | flops | bytes accessed | tf_op | source)
XLA Modules:
  0.0 880.5 jit_solution(11504680446807620341)
XLA Ops:
  8.2 1.3 convolution_convert_fusion
  9.5 79.2 %all-gather.5.cloned.1.call-done = bf16[1,1024,512]{2,1,0:T(8,128)(2,1)} async-done(((bf16[1,32,512]{2,1,0:T(8,128)(2,1)}), bf16[1,1024,512]{2,1,0:T(8,128)(2,1)}) %all-gather.5.cloned.1.call-update) | async-done | bytes 1048592 | tf_op jit(solution)/shard_map/all_gather | solution.py:23
  88.7 1.4 fusion.117
  90.0 1.6 fusion.118
  91.6 1.5 fusion.119
  100.0 1.0 convolution_dynamic-update-slice_fusion.4
  102.0 1.0 convolution_dynamic-update-slice_fusion.2
  105.0 2.9 copy.27
  107.9 7.5 all-to-all-start.1
  116.1 139.8 %all-gather.7.cloned.1.call-done = bf16[1,1024,512]{2,1,0:T(8,128)(2,1)} async-done(((bf16[1,32,512]{2,1,0:T(8,128)(2,1)}), bf16[1,1024,512]{2,1,0:T(8,128)(2,1)}) %all-gather.7.cloned.1.call-update) | async-done | bytes 1048592 | tf_op jit(solution)/shard_map/all_gather | solution.py:24
  255.9 1.4 convolution_convert_fusion.2
  257.3 1.3 convolution_convert_fusion.3
  258.7 1.3 convolution_convert_fusion.4
  266.5 1.0 convolution_dynamic-update-slice_fusion.12
  271.6 1.0 convolution_dynamic-update-slice_fusion.8
  272.6 2.9 copy.26
  275.6 7.6 all-to-all-start
  283.6 1.3 convolution_multiply_fusion
  287.7 417.7 %all-reduce.3.cloned.1.call-done = f32[512,512]{1,0:T(8,128)} async-done(((f32[512,512]{1,0:T(8,128)}), f32[512,512]{1,0:T(8,128)}) %all-reduce.3.cloned.1.call-update) | async-done | bytes 1048592 | tf_op jit(solution)/shard_map/psum | solution.py:67
  710.1 1.8 copy.28
  711.8 2.4 reduce_sum.179
  714.2 2.4 reduce_sum.178
  716.6 155.1 %all-reduce.5.cloned.1.call-done = f32[512,512]{1,0:T(8,128)} async-done(((f32[512,512]{1,0:T(8,128)}), f32[512,512]{1,0:T(8,128)}) %all-reduce.5.cloned.1.call-update) | async-done | bytes 1048592 | tf_op jit(solution)/shard_map/psum | solution.py:67
  871.7 2.3 copy.60
  (155 shorter events, 29.4 us)
Async XLA Ops:
  7.2 84.4 %copy-start.25 = (bf16[1,128,512]{2,1,0:T(8,128)(2,1)S(1)}, bf16[1,128,512]{2,1,0:T(8,128)(2,1)}, u32[]{:S(2)}) copy-start(bf16[1,128,512]{2,1,0:T(8,128)(2,1)} %param.5) | copy-start | bytes 393220
  7.2 81.5 %all-gather.5.cloned.1.call-start = ((), (), s32[]{:S(2)}) async-start(), calls=%async_computation.4 | async-start | bytes 1081344 | tf_op jit(solution)/shard_map/all_gather | solution.py:23
  90.0 6.9 copy-start.9
  91.6 6.3 copy-start.7
  93.5 6.5 copy-start.3
  95.0 9.0 %copy-start.11 = (f32[128,1024]{1,0:T(8,128)}, f32[128,1024]{1,0:T(8,128)S(1)}, u32[]{:S(2)}) copy-start(f32[128,1024]{1,0:T(8,128)S(1)} %get-tuple-element.21) | copy-start | bytes 1572868
  97.0 164.4 %copy-start.43 = (f32[128]{0:T(128)}, f32[128]{0:T(128)S(1)}, u32[]{:S(2)}) copy-start(f32[128]{0:T(128)S(1)} %log_add_fusion) | copy-start | bytes 1540
  107.9 167.7 %all-to-all-start.1 = ((f32[32,32,512]{2,1,0:T(8,128)}), f32[32,32,512]{2,1,0:T(8,128)}, u32[]{:S(2)}, u32[]{:S(2)}) async-start(f32[32,32,512]{2,1,0:T(8,128)} %bitcast.63), calls=%async_computation.1 | async-start | bytes 4194304 | tf_op jit(solution)/shard_map/all_to_all | solution.py:60
  115.4 140.5 %all-gather.7.cloned.1.call-start = ((), (), s32[]{:S(2)}) async-start(), calls=%async_computation.5 | async-start | bytes 1081344 | tf_op jit(solution)/shard_map/all_gather | solution.py:24
  275.5 7.8 copy-start.29
  275.5 7.8 copy-start.31
  275.6 7.8 copy-start.33
  275.6 7.8 copy-start.35
  275.6 7.8 copy-start.37
  275.6 7.8 copy-start.39
  275.6 7.8 copy-start.41
  275.6 7.8 copy-start.42
  275.6 8.0 copy-start.27
  275.6 438.6 %all-to-all-start = ((f32[32,32,512]{2,1,0:T(8,128)}), f32[32,32,512]{2,1,0:T(8,128)}, u32[]{:S(2)}, u32[]{:S(2)}) async-start(f32[32,32,512]{2,1,0:T(8,128)} %bitcast.64), calls=%async_computation | async-start | bytes 4194304 | tf_op jit(solution)/shard_map/all_to_all | solution.py:59
  283.3 422.1 %all-reduce.3.cloned.1.call-start = ((), (), s32[]{:S(2)}) async-start(), calls=%async_computation.2 | async-start | bytes 2097152 | tf_op jit(solution)/shard_map/psum | solution.py:67
  284.9 421.5 %copy-start.16 = (bf16[128,1024]{1,0:T(8,128)(2,1)S(1)}, bf16[128,1024]{1,0:T(8,128)(2,1)}, u32[]{:S(2)}) copy-start(bf16[128,1024]{1,0:T(8,128)(2,1)} %copy-done.15) | copy-start | bytes 786436
  284.9 422.4 %copy-start.20 = (bf16[128,1024]{1,0:T(8,128)(2,1)S(1)}, bf16[128,1024]{1,0:T(8,128)(2,1)}, u32[]{:S(2)}) copy-start(bf16[128,1024]{1,0:T(8,128)(2,1)} %copy-done.19) | copy-start | bytes 786436
  284.9 586.8 %all-reduce.5.cloned.1.call-start = ((), (), s32[]{:S(2)}) async-start(), calls=%async_computation.3 | async-start | bytes 2097152 | tf_op jit(solution)/shard_map/psum | solution.py:67
  285.8 423.3 %copy-start.24 = (bf16[128,1024]{1,0:T(8,128)(2,1)S(1)}, bf16[128,1024]{1,0:T(8,128)(2,1)}, u32[]{:S(2)}) copy-start(bf16[128,1024]{1,0:T(8,128)(2,1)} %copy-done.23) | copy-start | bytes 786436
  (27 other events, 87.1 us)
Sparse Core Ops, SparseCore 0:
  11.2 77.4 all-gather.4
  119.4 136.5 all-gather.6
  287.6 417.7 all-reduce.2
  708.4 163.2 all-reduce.4
